TPU v7x, 32 devices: a whole 2x2x4 slice. The times are simulated.
32 devices in a mesh: seq: 8 (over z, x), tp: 4 (over y, core).
Axes of the slice: x: 2, y: 2, z: 4, core: 2. Of those that a mesh axis runs over, the one named last changes fastest.
Arguments:
- tokens: bfloat16 [16384, 768], P('seq'), may hold values from -6 to 6
- cotangent: bfloat16 [16384, 768], P('seq'), may hold values from -6 to 6
- lengths: int32 [256], replicated, may hold values from 1 to 128, 16384 in all
- w_qkv: bfloat16 [3, 768, 768], P(None, None, 'tp'), may hold values from -0.21875 to 0.21875
- qv_bias: float32 [2, 768], P(None, 'tp'), may hold values from -3 to 3
- w_out: bfloat16 [768, 768], P('tp'), may hold values from -0.625 to 0.625
- out_bias: float32 [768], replicated, may hold values from -2 to 2
- gain_first: float32 [768], replicated, may hold values from 0.5 to 1.5
- shift_first: float32 [768], replicated, may hold values from -2 to 2
- w_up: bfloat16 [768, 3072], P(None, 'tp'), may hold values from -0.21875 to 0.21875
- up_bias: float32 [3072], P('tp'), may hold values from -3 to 3
- w_down: bfloat16 [3072, 768], P('tp'), may hold values from -0.15625 to 0.15625
- down_bias: float32 [768], replicated, may hold values from -2 to 2
- gain_second: float32 [768], replicated, may hold values from 0.5 to 1.5
- shift_second: float32 [768], replicated, may hold values from -2 to 2
Outputs:
- activations: bfloat16 [16384, 768], P('seq')
- input_grad: float32 [16384, 768], P('seq')
- grad_qkv: float32 [3, 768, 768], P(None, None, 'tp')
- grad_qv_bias: float32 [2, 768], P(None, 'tp')
- grad_w_out: float32 [768, 768], P('tp')
- grad_out_bias: float32 [768], replicated
- grad_gain_first: float32 [768], replicated
- grad_shift_first: float32 [768], replicated
- grad_w_up: float32 [768, 3072], P(None, 'tp')
- grad_up_bias: float32 [3072], P('tp')
- grad_w_down: float32 [3072, 768], P('tp')
- grad_down_bias: float32 [768], replicated
- grad_gain_second: float32 [768], replicated
- grad_shift_second: float32 [768], replicated
Inputs may be any that keep to these rules, and one draw needn't show every extreme that they name: lengths of the 256 sentences in order; they sum to 16384, and the longest is exactly 128.
All inputs are finite; a program needn't handle non-finite values.
Results may differ from a plain program's by a relative error of at most 0.012.
The roundings to bfloat16 on the way count: a program that leaves them out, or rounds other values in their place, can miss the bound.
Values may be sent and summed in bfloat16 or wider, within the bound.
No kernel may reach another device: no remote copies, remote signals or barrier semaphores. Data moves between devices by JAX's collectives and lax.ppermute only.
A program may use at most 128 MiB of HBM per device.

v0:
```python
import jax
import jax.numpy as jnp
from jax import lax
from jax.sharding import PartitionSpec as P

HEAD = 64
MOST = 128


EPS = 1e-12


def padded(block, sides, width):
    for axis, dim in sides:
        count = lax.axis_size(axis)
        forward = [(i, i + 1) for i in range(count - 1)]
        backward = [(target, source) for source, target in forward]
        low = lax.ppermute(
            lax.slice_in_dim(block, block.shape[dim] - width, None, axis=dim), axis, forward
        )
        high = lax.ppermute(lax.slice_in_dim(block, 0, width, axis=dim), axis, backward)
        block = jnp.concatenate([low, block, high], axis=dim)
    return block


def product(left, right):
    return jnp.dot(left, right, preferred_element_type=jnp.float32)


def product_over(left, right):
    return lax.dot_general(
        left, right, (((0,), (0,)), ((), ())), preferred_element_type=jnp.float32
    )


def product_back(left, right):
    return lax.dot_general(
        left, right, (((1,), (1,)), ((), ())), preferred_element_type=jnp.float32
    )


def norm_rows(resid, scale_row, shift_row):
    row_mean = jnp.mean(resid, -1, keepdims=True)
    centred = resid - row_mean
    variance = jnp.mean(centred * centred, -1, keepdims=True)
    inv_std = lax.rsqrt(variance + EPS)
    normed = centred * inv_std
    return (normed * scale_row + shift_row, normed, inv_std)


def norm_back(grad_in, normed, inv_std, scale_row):
    scaled = grad_in * scale_row
    inner = (
        scaled
        - jnp.mean(scaled, -1, keepdims=True)
        - normed * jnp.mean(scaled * normed, -1, keepdims=True)
    )
    return (inv_std * inner, jnp.sum(grad_in * normed, 0), jnp.sum(grad_in, 0))


def attention_weights(query_blk, key_blk, query_sent, key_sent):
    scores = jnp.einsum(
        "qhd,khd->hqk", query_blk, key_blk, preferred_element_type=jnp.float32
    ) * HEAD ** (-0.5)
    scores = jnp.where((query_sent[:, None] == key_sent[None, :])[None], scores, -1e30)
    row_max = jnp.max(scores, -1, keepdims=True)
    raised = jnp.exp(scores - row_max)
    return raised / jnp.sum(raised, -1, keepdims=True)


def gelu_exact(pre_act):
    return jax.nn.gelu(pre_act, approximate=False)


def on_device(
    tokens,
    cotangent,
    lengths,
    w_qkv,
    qv_bias,
    w_out,
    out_bias,
    gain_first,
    shift_first,
    w_up,
    up_bias,
    w_down,
    down_bias,
    gain_second,
    shift_second,
):
    rows_here = tokens.shape[0]
    head_cols = w_qkv.shape[2]
    head_count = head_cols // HEAD
    block_rows = min(512, rows_here)
    window = block_rows + 2 * MOST
    block_count = rows_here // block_rows
    inputs = tokens.astype(jnp.float32)
    queries = (product(tokens, w_qkv[0]) + qv_bias[0]).astype(jnp.bfloat16)
    keys_here = product(tokens, w_qkv[1]).astype(jnp.bfloat16)
    values_here = (product(tokens, w_qkv[2]) + qv_bias[1]).astype(jnp.bfloat16)
    key_value = jnp.stack([keys_here, values_here])
    extended = padded(key_value, (("seq", 1),), MOST)
    all_rows = rows_here * lax.axis_size("seq")
    places = (
        lax.axis_index("seq") * rows_here + jnp.arange(rows_here + 2 * MOST, dtype=jnp.int32) - MOST
    )
    sent_ends = jnp.cumsum(lengths)
    passed = jnp.sum((sent_ends[None, :] <= places[:, None]).astype(jnp.int32), 1)
    sent_of = jnp.where((places < 0) | (places >= all_rows), -1, passed)

    def block_inputs(block_index):
        first_row = block_index * block_rows
        query_blk = lax.dynamic_slice_in_dim(queries, first_row, block_rows, 0).reshape(
            block_rows, head_count, HEAD
        )
        pair_blk = lax.dynamic_slice_in_dim(extended, first_row, window, 1).reshape(
            2, window, head_count, HEAD
        )
        query_sent = lax.dynamic_slice_in_dim(sent_of, first_row + MOST, block_rows, 0)
        key_sent = lax.dynamic_slice_in_dim(sent_of, first_row, window, 0)
        weights = attention_weights(query_blk, pair_blk[0], query_sent, key_sent)
        return (query_blk, pair_blk, weights)

    def attend(block_index):
        query_blk, pair_blk, weights = block_inputs(block_index)
        mixed_blk = jnp.einsum(
            "hqk,khd->qhd",
            weights.astype(jnp.bfloat16),
            pair_blk[1],
            preferred_element_type=jnp.float32,
        )
        return mixed_blk.reshape(block_rows, head_cols)

    blocks = jnp.arange(block_count, dtype=jnp.int32)
    mixed = lax.map(attend, blocks).reshape(rows_here, head_cols).astype(jnp.bfloat16)
    cot_full = cotangent.astype(jnp.float32)
    attn = lax.psum(product(mixed, w_out), "tp") + out_bias
    first_out, normed_first, inv_first = norm_rows(inputs + attn, gain_first, shift_first)
    first_low = first_out.astype(jnp.bfloat16)
    upward = product(first_low, w_up) + up_bias
    activated = gelu_exact(upward).astype(jnp.bfloat16)
    downward = lax.psum(product(activated, w_down), "tp") + down_bias
    result, normed_second, inv_second = norm_rows(first_out + downward, gain_second, shift_second)
    result_low = result.astype(jnp.bfloat16)
    grad_res2, grad_gain2, grad_shift2 = norm_back(cot_full, normed_second, inv_second, gain_second)
    grad_down_low = grad_res2.astype(jnp.bfloat16)
    grad_down = product_over(activated, grad_down_low)
    grad_down_bias = jnp.sum(grad_down_low.astype(jnp.float32), 0)
    grad_act = product_back(grad_down_low, w_down)
    unused_value, gelu_pull = jax.vjp(gelu_exact, upward)
    grad_up_low = gelu_pull(grad_act)[0].astype(jnp.bfloat16)
    grad_up = product_over(first_low, grad_up_low)
    grad_up_bias = jnp.sum(grad_up_low.astype(jnp.float32), 0)
    grad_first = lax.psum(product_back(grad_up_low, w_up), "tp") + grad_res2
    grad_res1, grad_gain1, grad_shift1 = norm_back(grad_first, normed_first, inv_first, gain_first)
    grad_attn_low = grad_res1.astype(jnp.bfloat16)
    grad_out = product_over(mixed, grad_attn_low)
    grad_out_bias = jnp.sum(grad_attn_low.astype(jnp.float32), 0)
    grad_mixed = product_back(grad_attn_low, w_out).astype(jnp.bfloat16)

    def attend_back(carried, block_index):
        query_blk, pair_blk, weights = block_inputs(block_index)
        first_row = block_index * block_rows
        grad_blk = lax.dynamic_slice_in_dim(grad_mixed, first_row, block_rows, 0).reshape(
            block_rows, head_count, HEAD
        )
        grad_values = jnp.einsum(
            "hqk,qhd->khd",
            weights.astype(jnp.bfloat16),
            grad_blk,
            preferred_element_type=jnp.float32,
        )
        grad_weights = jnp.einsum(
            "qhd,khd->hqk", grad_blk, pair_blk[1], preferred_element_type=jnp.float32
        )
        grad_scores = (
            weights * (grad_weights - jnp.sum(weights * grad_weights, -1, keepdims=True))
        ).astype(jnp.bfloat16)
        grad_query = jnp.einsum(
            "hqk,khd->qhd", grad_scores, pair_blk[0], preferred_element_type=jnp.float32
        ) * HEAD ** (-0.5)
        grad_keys = jnp.einsum(
            "hqk,qhd->khd", grad_scores, query_blk, preferred_element_type=jnp.float32
        ) * HEAD ** (-0.5)
        grad_pair = jnp.stack([grad_keys, grad_values]).reshape(2, window, head_cols)
        current = lax.dynamic_slice_in_dim(carried, first_row, window, 1)
        carried = lax.dynamic_update_slice_in_dim(carried, current + grad_pair, first_row, 1)
        return (carried, grad_query.reshape(block_rows, head_cols))

    grad_ext, grad_queries = lax.scan(
        attend_back, jnp.zeros((2, rows_here + 2 * MOST, head_cols), jnp.float32), blocks
    )
    grad_queries = grad_queries.reshape(rows_here, head_cols).astype(jnp.bfloat16)
    rims = jnp.concatenate([grad_ext[:, :MOST], grad_ext[:, rows_here + MOST :]], 1)
    arrived = padded(rims.astype(jnp.bfloat16), (("seq", 1),), MOST).astype(rims.dtype)
    grad_pair = grad_ext[:, MOST : MOST + rows_here]
    grad_pair = grad_pair + jnp.pad(arrived[:, :MOST], ((0, 0), (0, rows_here - MOST), (0, 0)))
    grad_pair = grad_pair + jnp.pad(arrived[:, 3 * MOST :], ((0, 0), (rows_here - MOST, 0), (0, 0)))
    grad_pair = grad_pair.astype(jnp.bfloat16)
    grad_stack = jnp.stack([grad_queries, grad_pair[0], grad_pair[1]])
    grad_qkv = jnp.einsum("td,jtc->jdc", tokens, grad_stack, preferred_element_type=jnp.float32)
    grad_qv_bias = jnp.stack(
        [jnp.sum(grad_queries.astype(jnp.float32), 0), jnp.sum(grad_pair[1].astype(jnp.float32), 0)]
    )
    input_part = jnp.einsum("jtc,jdc->td", grad_stack, w_qkv, preferred_element_type=jnp.float32)
    input_grad = lax.psum(input_part, "tp") + grad_res1
    (
        grad_qkv,
        grad_qv_bias,
        grad_out,
        grad_out_bias,
        grad_gain1,
        grad_shift1,
        grad_up,
        grad_up_bias,
        grad_down,
        grad_down_bias,
        grad_gain2,
        grad_shift2,
    ) = lax.psum(
        (
            grad_qkv,
            grad_qv_bias,
            grad_out,
            grad_out_bias,
            grad_gain1,
            grad_shift1,
            grad_up,
            grad_up_bias,
            grad_down,
            grad_down_bias,
            grad_gain2,
            grad_shift2,
        ),
        "seq",
    )
    return (
        result_low,
        input_grad,
        grad_qkv,
        grad_qv_bias,
        grad_out,
        grad_out_bias,
        grad_gain1,
        grad_shift1,
        grad_up,
        grad_up_bias,
        grad_down,
        grad_down_bias,
        grad_gain2,
        grad_shift2,
    )


def solution(mesh):
    placed = (
        P("seq", None),
        P("seq", None),
        P(),
        P(None, None, "tp"),
        P(None, "tp"),
        P("tp", None),
        P(),
        P(),
        P(),
        P(None, "tp"),
        P("tp"),
        P("tp", None),
        P(),
        P(),
        P(),
    )
    return jax.shard_map(
        on_device,
        mesh=mesh,
        in_specs=placed,
        out_specs=(
            P("seq", None),
            P("seq", None),
            P(None, None, "tp"),
            P(None, "tp"),
            P("tp", None),
            P(),
            P(),
            P(),
            P(None, "tp"),
            P("tp"),
            P("tp", None),
            P(),
            P(),
            P(),
        ),
        check_vma=False,
    )
```

profile of v0, /device:TPU:0, one launch (start us, length us, event | category | flops | bytes accessed | tf_op | source)
XLA Modules:
  0.0 996.8 jit_solution(17207724298371998056)
XLA Ops:
  13.7 4.8 collective-permute-start
  28.4 52.1 %while.26 = (s32[]{:T(128)}, bf16[4,512,192]{1,2,0:T(8,128)(2,1)}, s32[4]{0:T(128)S(1)}, bf16[2,2304,192]{1,2,0:T(8,128)(2,1)S(1)}, s32[2304]{0:T(1024)S(1)}, /*...) while((s32[]{:T(128)}, bf16[4,512,192]{1,2,0:T(8,128)(2,1)}, ...), condition=%wide.region_6.7_spmd, body=%wide.region_3.6_spmd.sunk | while | flops 309461760 | bytes 13201190 | solution.py:136
  31.9 5.5 fusion.130
  44.9 5.5 fusion.130
  57.9 5.5 fusion.130
  70.9 5.5 fusion.130
  82.6 4.7 fusion.71
  87.9 121.6 %all-reduce.10.cloned.1.call-done = f32[2048,768]{1,0:T(8,128)} async-done(((f32[2048,768]{1,0:T(8,128)}), f32[2048,768]{1,0:T(8,128)}) %all-reduce.10.cloned.1.call-update) | async-done | bytes 6291472 | tf_op jit(solution)/shard_map/psum | solution.py:138
  209.5 4.6 fusion.66
  216.7 18.3 %multiply_convert_fusion.1 = (bf16[2048,768]{1,0:T(8,128)(2,1)S(1)}, f32[2048,768]{1,0:T(8,128)}, f32[2048,768]{1,0:T(8,128)}) fusion(f32[768]{0:T(1024)S(1)} %copy-done.37, bf16[2048,768]{1,0:T(8,128)(2,1)S(1)} %fusion.35, bf16[768,768]{1,0:T(8,128)(2,1)S(1)} %copy-done), kind=kOutput, calls=%fused_computation.64 | convolution fusion | flops 2519728128 | bytes 20057088 | tf_op jit(solution)/shard_map/dot_general | solution.py:27
  236.8 4.4 fusion.72
  241.5 119.7 %all-reduce.12.cloned.1.call-done = f32[2048,768]{1,0:T(8,128)} async-done(((f32[2048,768]{1,0:T(8,128)}), f32[2048,768]{1,0:T(8,128)}) %all-reduce.12.cloned.1.call-update) | async-done | bytes 6291472 | tf_op jit(solution)/shard_map/psum | solution.py:143
  361.2 5.7 fusion.64
  372.4 4.5 convert_reduce_fusion.1
  376.9 9.5 convert_reduce_fusion.2
  388.1 4.5 fusion.73
  393.0 119.7 %all-reduce.14.cloned.1.call-done = f32[2048,768]{1,0:T(8,128)} async-done(((f32[2048,768]{1,0:T(8,128)}), f32[2048,768]{1,0:T(8,128)}) %all-reduce.14.cloned.1.call-update) | async-done | bytes 6291472 | tf_op jit(solution)/shard_map/psum | solution.py:155
  512.7 8.7 multiply_reduce_fusion.1
  521.4 5.2 convert_reduce_fusion.3
  534.3 66.5 %while.27 = (s32[]{:T(128)}, f32[2,2304,192]{1,2,0:T(8,128)}, bf16[4,512,192]{1,2,0:T(8,128)(2,1)}, s32[4]{0:T(128)S(1)}, bf16[2048,192]{0,1:T(8,128)(2,1)}, /*i...) while((s32[]{:T(128)}, f32[2,2304,192]{1,2,0:T(8,128)}, ...), condition=%wide.region_22.23_spmd, body=%wide.region_18.22_spmd.sunk | while | flops 771636480 | bytes 92360576 | solution.py:191
  537.2 4.0 fusion.142
  553.8 4.0 fusion.142
  570.4 4.0 fusion.142
  587.0 4.0 fusion.142
  615.1 5.7 convolution_bitcast_fusion
  621.2 7.1 fusion.74
  628.2 7.0 fusion.57
  635.2 4.5 fusion.54
  644.7 36.7 %all-reduce.2 = (f32[2,192]{1,0:T(2,128)}, f32[768]{0:T(1024)}, f32[768]{0:T(1024)}, f32[768]{0:T(1024)}, f32[768]{0:T(1024)}, /*index=5*/f32[768]{0:T(1024)}, f32[768]{0:T(1024)}, f32[768]{0:T(1024)}) all-reduce(f32[2,192]{1,0:T(2,128)S(1)} %pad_maximum_fusion.9, f32[768]{0:T(1024)S(1)} %copy-done.27, ...), channel_id=1, replica_groups=mesh['seq'=8,'tp'=4] {'seq'}, use_global_device_ids=true, to_apply=%region_27.28 | all-reduce | flops 5760 | bytes 46080 | tf_op jit(solution)/shard_map/psum | solution.py:221
  681.3 59.4 %all-reduce.16.cloned.1.call-done = f32[2048,768]{1,0:T(8,128)} async-done(((f32[2048,768]{1,0:T(8,128)}), f32[2048,768]{1,0:T(8,128)}) %all-reduce.16.cloned.1.call-update) | async-done | bytes 6291472 | tf_op jit(solution)/shard_map/psum | solution.py:207
  740.8 8.1 add.249
  748.9 233.4 %all-reduce.18.cloned.1.call-done = (f32[3,768,192]{1,2,0:T(8,128)}, f32[192,768]{1,0:T(8,128)}, f32[768,768]{1,0:T(8,128)}, f32[768,768]{1,0:T(8,128)}) async-done(((f32[3,768,192]{1,2,0:T(8,128)}, f32[192,768]{1,0:T(8,128)}, f32[768,768]{1,0:T(8,128)}, f32[768,768]{1,0:T(8,128)}), (f32[3,768,192]{1,2,0:T(8,128)}, f32[192,768]{1,0:T(8,128)}, f32[768,768]{1,0:T(8,128)}, ...) | async-done | bytes 7077904 | tf_op jit(solution)/shard_map/psum | solution.py:221
  (248 shorter events, 140.6 us)
Async XLA Ops:
  7.2 209.5 %copy-start = (bf16[768,768]{1,0:T(8,128)(2,1)S(1)}, bf16[768,768]{1,0:T(8,128)(2,1)}, u32[]{:S(2)}) copy-start(bf16[768,768]{1,0:T(8,128)(2,1)} %param.28) | copy-start | bytes 3538948
  7.2 4.4 copy-start.36
  7.2 202.2 %all-reduce.10.cloned.1.call-start = ((), (), s32[]{:S(2)}) async-start(), calls=%async_computation | async-start | bytes 12582912 | tf_op jit(solution)/shard_map/psum | solution.py:138
  7.3 4.4 copy-start.16
  8.1 11.8 %copy-start.33 = (s32[256]{0:T(256)S(1)}, s32[256]{0:T(256)}, u32[]{:S(2)}) copy-start(s32[256]{0:T(256)} %param.21) | copy-start | bytes 3076
  13.7 12.2 %collective-permute-start = (bf16[2,128,192]{1,2,0:T(8,128)(2,1)S(1)}, bf16[2,128,192]{1,2,0:T(8,128)(2,1)S(1)}, u32[]{:S(2)}, u32[]{:S(2)}) collective-permute-start(bf16[2,128,192]{1,2,0:T(8,128)(2,1)S(1)} %get-tuple-element.270), channel_id=1, source_target_pairs={{0,4},{4,8},{8,12},{12,16},{16,20},{20,24},{24,28},{1,5},{5,9},{9,... | collective-permute-start | bytes 294920 | tf_op jit(solution)/shard_map/ppermute | solution.py:18
  18.6 7.3 collective-permute-start.1
  82.6 126.9 %copy-start.31 = (f32[768]{0:T(1024)S(1)}, f32[768]{0:T(1024)}, u32[]{:S(2)}) copy-start(f32[768]{0:T(1024)} %param.25) | copy-start | bytes 9220
  87.3 273.9 %all-reduce.12.cloned.1.call-start = ((), (), s32[]{:S(2)}) async-start(), calls=%async_computation.1 | async-start | bytes 12582912 | tf_op jit(solution)/shard_map/psum | solution.py:143
  216.7 18.3 %copy-start.13 = (bf16[2048,768]{1,0:T(8,128)(2,1)}, bf16[2048,768]{1,0:T(8,128)(2,1)S(1)}, u32[]{:S(2)}) copy-start(bf16[2048,768]{1,0:T(8,128)(2,1)S(1)} %fusion.35) | copy-start | bytes 9437188
  216.7 20.1 %copy-start.34 = (bf16[768,768]{1,0:T(8,128)(2,1)S(1)}, bf16[768,768]{1,0:T(8,128)(2,1)}, u32[]{:S(2)}) copy-start(bf16[768,768]{1,0:T(8,128)(2,1)} %param.30) | copy-start | bytes 3538948
  241.3 120.0 %copy-start.32 = (f32[768]{0:T(1024)S(1)}, f32[768]{0:T(1024)}, u32[]{:S(2)}) copy-start(f32[768]{0:T(1024)} %param.31) | copy-start | bytes 9220
  241.3 271.4 %all-reduce.14.cloned.1.call-start = ((), (), s32[]{:S(2)}) async-start(), calls=%async_computation.2 | async-start | bytes 12582912 | tf_op jit(solution)/shard_map/psum | solution.py:155
  367.8 4.6 copy-start.29
  368.8 8.1 slice-start
  372.4 4.5 copy-start.35
  372.4 4.5 slice-start.1
  376.9 9.5 copy-start.7
  392.7 348.1 %all-reduce.16.cloned.1.call-start = ((), (), s32[]{:S(2)}) async-start(), calls=%async_computation.3 | async-start | bytes 12582912 | tf_op jit(solution)/shard_map/psum | solution.py:207
  521.4 7.9 copy-start.20
  541.1 3.8 copy-start.3
  557.7 3.8 copy-start.3
  591.0 3.8 copy-start.3
  603.0 7.0 collective-permute-start.2
  606.4 6.5 collective-permute-start.3
  620.9 361.5 %all-reduce.18.cloned.1.call-start = ((), (), s32[]{:S(2)}) async-start(), calls=%async_computation.4 | async-start | bytes 14155776 | tf_op jit(solution)/shard_map/psum | solution.py:221
  621.2 7.1 copy-start.15
  628.2 7.0 copy-start.10
  635.2 4.5 copy-start.17
  982.3 4.9 copy-start.19
  982.3 6.3 copy-start.18
  982.3 7.7 copy-start.1
  (27 other events, 47.9 us)
Sparse Core Ops, SparseCore 0:
  87.4 121.9 all-reduce.9
  241.4 119.7 all-reduce.11
  392.8 119.7 all-reduce.13
  621.0 119.7 all-reduce.15
  746.2 236.0 all-reduce.17
where the time goes:
time: 1000 us; the launch traced here: 997 us
  waiting for transfers between devices  657 us (66%)
  matrix products  153 us (15%)
  other arithmetic  59.1 us (6%)
  local copies, waits for them, and re-layouts  59 us (6%)
  blocking collectives  36.7 us (4%)
  between operations  14.5 us (1%)
  starting transfers between devices  12.2 us (1%)
    psum x1, waiting for transfers between devices, on_device(): lax.psum((grad_qkv, grad_qv_bias, grad_out, grad_out_bias, grad_gain1, gr...  233 us
    psum x1, waiting for transfers between devices, on_device(): attn = lax.psum(product(mixed, w_out), 'tp') + out_bias  122 us
    psum x1, waiting for transfers between devices, on_device(): downward = lax.psum(product(activated, w_down), 'tp') + down_bias  120 us
    psum x1, waiting for transfers between devices, on_device(): grad_first = lax.psum(product_back(grad_up_low, w_up), 'tp') + grad_res2  120 us
    psum x1, waiting for transfers between devices, on_device(): input_grad = lax.psum(input_part, 'tp') + grad_res1  59.4 us
    sub x8, matrix products, attention_weights(): raised = jnp.exp(scores - row_max)  38.1 us
    psum x1, blocking collectives, on_device(): lax.psum((grad_qkv, grad_qv_bias, grad_out, grad_out_bias, grad_gain1, gr...  36.7 us
    dot_general x6, matrix products, product(): return jnp.dot(left, right, preferred_element_type=jnp.float32)  36.1 us
  transfers between devices with their start and end apart: 9, of which 6 were waited for; matrix products, arithmetic and copies ran while one was open for 4% of the time, Pallas kernels for 0%

commit v1 on v0

v1 whole, which is shorter than its diff:
```python
import jax
import jax.numpy as jnp
from jax import lax
from jax.experimental import pallas as pl
from jax.experimental.pallas import tpu as pltpu
from jax.sharding import PartitionSpec as P

HEAD = 64
MOST = 128
EPS = 1e-12
BF = jnp.bfloat16
F32 = jnp.float32
MIB = 1024 * 1024


def nn(left, right):
    return lax.dot_general(left, right, (((1,), (0,)), ((), ())), preferred_element_type=F32)


def nt(left, right):
    return lax.dot_general(left, right, (((1,), (1,)), ((), ())), preferred_element_type=F32)


def tn(left, right):
    return lax.dot_general(left, right, (((0,), (0,)), ((), ())), preferred_element_type=F32)


VMEM = pl.BlockSpec(memory_space=pltpu.VMEM)
SMEM = pl.BlockSpec(memory_space=pltpu.SMEM)


ANY = pl.BlockSpec(memory_space=pl.ANY)


def call(body, outs, specs, name, args, after=(), scratch=(), limit=56):
    given = len(args)

    def whole(*refs):
        body(*refs[:given], *refs[given + len(after) :])

    return pl.pallas_call(
        whole,
        out_shape=[jax.ShapeDtypeStruct(shape, dtype) for shape, dtype in outs],
        in_specs=list(specs) + [ANY] * len(after),
        out_specs=[VMEM] * len(outs),
        scratch_shapes=list(scratch),
        name=name,
        cost_estimate=pl.CostEstimate(flops=0, bytes_accessed=0, transcendentals=0),
        compiler_params=pltpu.CompilerParams(vmem_limit_bytes=limit * MIB),
    )(*args, *after)


def stack_heads(block, heads):
    lane = lax.broadcasted_iota(jnp.int32, block.shape, 1) // HEAD
    zero = jnp.zeros_like(block)
    return jnp.concatenate([jnp.where(lane == h, block, zero) for h in range(heads)], 0)


def pick_heads(stacked, heads):
    rows = stacked.shape[0] // heads
    lane = lax.broadcasted_iota(jnp.int32, (rows, stacked.shape[1]), 1) // HEAD
    out = stacked[:rows]
    for h in range(1, heads):
        out = jnp.where(lane == h, stacked[h * rows : (h + 1) * rows], out)
    return out


def attend_body(
    place, tokens, low, high, wt, bias, ids_col, ids_row, q_out, k_out, v_out, p_out, mixed_out
):
    rows = tokens.shape[0]
    cols = wt.shape[1]
    heads = cols // HEAD
    quarter = mixed_out.shape[1]
    scale = jnp.asarray(HEAD**-0.5, BF)

    def project(source, first, size, target, with_q):
        block = source[pl.ds(first, size), :]
        k_out[pl.ds(target, size), :] = nt(block, wt[1]).astype(BF)
        v_out[pl.ds(target, size), :] = (nt(block, wt[2]) + bias[1:2, :]).astype(BF)
        if with_q:
            q_out[pl.ds(first, size), :] = (nt(block, wt[0]) + bias[0:1, :]).astype(BF)

    project(low, 0, MOST, 0, False)
    project(high, 0, MOST, rows + MOST, False)
    step = 256

    @pl.loop(0, rows // step)
    def _(i):
        first = pl.multiple_of(i * step, step)
        project(tokens, first, step, pl.multiple_of(first + MOST, MOST), True)

    @pl.loop(0, rows // MOST)
    def _(b):
        first = pl.multiple_of(b * MOST, MOST)
        q3 = stack_heads(q_out[pl.ds(first, MOST), :] * scale, heads)
        scores = nt(q3, k_out[pl.ds(first, 3 * MOST), :])
        mine = ids_col[pl.ds(pl.multiple_of(first + MOST, MOST), MOST), :]
        mask = mine == ids_row[:, pl.ds(first, 3 * MOST)]
        scores = jnp.where(jnp.concatenate([mask] * heads, 0), scores, -1e30)
        raised = jnp.exp(scores - jnp.max(scores, -1, keepdims=True))
        probs = raised * (1.0 / jnp.sum(raised, -1, keepdims=True))
        probs = probs.astype(BF)
        p_out[b] = probs
        mixed = pick_heads(nn(probs, v_out[pl.ds(first, 3 * MOST), :]), heads)
        per = quarter // MOST
        mixed_out[(b // per) ^ place[0], pl.ds(pl.multiple_of((b % per) * MOST, MOST), MOST), :] = (
            mixed.astype(BF)
        )


def attend(place, tokens, low, high, wt, bias, ids_col, ids_row, after=()):
    rows, cols = tokens.shape[0], wt.shape[1]
    heads = cols // HEAD
    ext = rows + 2 * MOST
    return call(
        attend_body,
        [
            ((rows, cols), BF),
            ((ext, cols), BF),
            ((ext, cols), BF),
            ((rows // MOST, heads * MOST, 3 * MOST), BF),
            ((4, rows // 4, cols), BF),
        ],
        [SMEM] + [VMEM] * 7,
        "attend",
        (place, tokens, low, high, wt, bias, ids_col, ids_row),
        after,
    )


def attend_back_body(place, q, k, v, probs, g0, g1, g2, g3, dq_out, dk_out, dv_out, grads):
    rows, cols = q.shape
    heads = cols // HEAD
    quarter = g0.shape[0]
    scale = jnp.asarray(HEAD**-0.5, BF)
    for rel, ref in enumerate((g0, g1, g2, g3)):
        grads[pl.ds(pl.multiple_of((place[0] ^ rel) * quarter, quarter), quarter), :] = ref[...]
    dk_out[...] = jnp.zeros_like(dk_out)
    dv_out[...] = jnp.zeros_like(dv_out)

    @pl.loop(0, rows // MOST)
    def _(b):
        first = pl.multiple_of(b * MOST, MOST)
        span = pl.ds(first, 3 * MOST)
        g_stack = stack_heads(grads[pl.ds(first, MOST), :], heads)
        q_stack = stack_heads(q[pl.ds(first, MOST), :] * scale, heads)
        p_low = probs[b]
        weights = p_low.astype(F32)
        grad_probs = nt(g_stack, v[span, :])
        inner = jnp.sum(weights * grad_probs, -1, keepdims=True)
        grad_scores = (weights * (grad_probs - inner)).astype(BF)
        dv_out[span, :] += tn(p_low, g_stack)
        dk_out[span, :] += tn(grad_scores, q_stack)
        dq = pick_heads(nn(grad_scores, k[span, :]), heads) * (HEAD**-0.5)
        dq_out[pl.ds(first, MOST), :] = dq.astype(BF)


def attend_back(place, q, k, v, probs, grads, after=()):
    rows, cols = q.shape
    ext = rows + 2 * MOST
    return call(
        attend_back_body,
        [((rows, cols), BF), ((ext, cols), F32), ((ext, cols), F32)],
        [SMEM] + [VMEM] * 8,
        "attend_back",
        (place, q, k, v, probs, *grads),
        after,
        scratch=[pltpu.VMEM((rows, cols), BF)],
    )


def project_back_body(place, tokens, dq, dk, dv, wt, dwt_out, keep_out, send_out):
    rows = tokens.shape[0]
    quarter = rows // 4
    for j, ref in enumerate((dq, dk, dv)):
        dwt_out[j] = tn(ref[...], tokens[...])
    for rel in range(4):
        here = pl.ds(pl.multiple_of((place[0] ^ rel) * quarter, quarter), quarter)
        part = nn(dq[here, :], wt[0]) + nn(dk[here, :], wt[1]) + nn(dv[here, :], wt[2])
        if rel % 2 == 0:
            keep_out[rel // 2] = part
        else:
            send_out[rel // 2] = part.astype(BF)


def project_back(place, tokens, dq, dk, dv, wt, after=()):
    rows, width = tokens.shape
    cols = wt.shape[1]
    return call(
        project_back_body,
        [
            ((3, cols, width), F32),
            ((2, rows // 4, width), F32),
            ((2, rows // 4, width), BF),
        ],
        [SMEM] + [VMEM] * 5,
        "project_back",
        (place, tokens, dq, dk, dv, wt),
        after,
    )


def gelu_parts(pre):
    size = jnp.abs(pre) * (0.5**0.5)
    bell = jnp.exp(-size * size)
    t = 1.0 / (1.0 + 0.3275911 * size)
    poly = 1.061405429
    for c in (-1.453152027, 1.421413741, -0.284496736, 0.254829592):
        poly = poly * t + c
    tail = 0.5 * poly * t * bell
    cdf = jnp.where(pre >= 0, 1.0 - tail, tail)
    return pre * cdf, cdf + pre * bell * 0.3989422804014327


def norm_stats(resid):
    centred = resid - jnp.mean(resid, -1, keepdims=True)
    inv = lax.rsqrt(jnp.mean(centred * centred, -1, keepdims=True) + EPS)
    return centred * inv, inv


def norm_pull(grad, normed, inv, gain):
    scaled = grad * gain
    return inv * (
        scaled
        - jnp.mean(scaled, -1, keepdims=True)
        - normed * jnp.mean(scaled * normed, -1, keepdims=True)
    )


def col_sum(values):
    return jnp.sum(values, 0, keepdims=True)


STEP = 256
OUT_BIAS, GAIN1, SHIFT1, DOWN_BIAS, GAIN2, SHIFT2 = range(6)


def forward_body(
    tokens, m0, m1, m2, m3, o0, o1, o2, o3, u0, u1, u2, u3, up_bias, rows_in,
    normed_out, inv_out, low_out, act_out, slope_out, first,
):
    attn = rows_in[OUT_BIAS : OUT_BIAS + 1, :]
    for m, o in ((m0, o0), (m1, o1), (m2, o2), (m3, o3)):
        attn = attn + nn(m[...], o[...])
    normed, inv = norm_stats(tokens[...].astype(F32) + attn)
    normed_out[...] = normed
    inv_out[...] = inv
    first[...] = (normed * rows_in[GAIN1 : GAIN1 + 1, :] + rows_in[SHIFT1 : SHIFT1 + 1, :]).astype(BF)
    low_out[...] = first[...]
    for rel, u in enumerate((u0, u1, u2, u3)):

        @pl.loop(0, u.shape[1] // STEP)
        def _(j):
            here = pl.ds(pl.multiple_of(j * STEP, STEP), STEP)
            pre = nn(first[...], u[:, here]) + up_bias[rel : rel + 1, here]
            act, slope = gelu_parts(pre)
            act_out[rel, :, here] = act.astype(BF)
            slope_out[rel, :, here] = slope


def forward(tokens, mixed, outs, ups, up_bias, rows_in, after=()):
    rows, width = tokens.shape
    hidden = ups[0].shape[1]
    return call(
        forward_body,
        [
            ((rows, width), F32),
            ((rows, 1), F32),
            ((rows, width), BF),
            ((4, rows, hidden), BF),
            ((4, rows, hidden), F32),
        ],
        [VMEM] * 15,
        "forward",
        (tokens, *mixed, *outs, *ups, up_bias, rows_in),
        after,
        scratch=[pltpu.VMEM((rows, width), BF)],
    )


def middle_body(
    normed1, act, w0, w1, w2, w3, cot, rows_in,
    result_out, res2_out, low_out, keep_out, send_out, sums_out,
):
    first = normed1[...] * rows_in[GAIN1 : GAIN1 + 1, :] + rows_in[SHIFT1 : SHIFT1 + 1, :]
    down = rows_in[DOWN_BIAS : DOWN_BIAS + 1, :]
    for rel, w in enumerate((w0, w1, w2, w3)):
        down = down + nn(act[rel], w[...])
    gain2 = rows_in[GAIN2 : GAIN2 + 1, :]
    normed, inv = norm_stats(first + down)
    result_out[...] = (normed * gain2 + rows_in[SHIFT2 : SHIFT2 + 1, :]).astype(BF)
    grad = cot[...].astype(F32)
    res2 = norm_pull(grad, normed, inv, gain2)
    res2_out[...] = res2
    low = res2.astype(BF)
    low_out[...] = low
    sums_out[0:1, :] = col_sum(grad * normed)
    sums_out[1:2, :] = col_sum(grad)
    sums_out[2:3, :] = col_sum(low.astype(F32))
    for rel in range(4):
        out = send_out if rel % 2 else keep_out
        out[rel // 2] = tn(act[rel], low_out[...]).astype(BF)


def middle(normed1, act, downs, cot, rows_in, after=()):
    rows, width = normed1.shape
    hidden = act.shape[2]
    return call(
        middle_body,
        [
            ((rows, width), BF),
            ((rows, width), F32),
            ((rows, width), BF),
            ((2, hidden, width), BF),
            ((2, hidden, width), BF),
            ((3, width), F32),
        ],
        [VMEM] * 8,
        "middle",
        (normed1, act, *downs, cot, rows_in),
        after,
    )


def backward_body(
    low2, res2, normed1, inv1, slope, w0, w1, w2, w3, u0, u1, u2, u3, o0, o1, o2, o3, rows_in,
    gup_out, res1_out, low_out, gm_out, sums_out, ups_out, total,
):
    total[...] = res2[...]
    for rel, (w, u) in enumerate(((w0, u0), (w1, u1), (w2, u2), (w3, u3))):

        @pl.loop(0, u.shape[1] // STEP)
        def _(j):
            here = pl.ds(pl.multiple_of(j * STEP, STEP), STEP)
            grad_act = nt(low2[...], w[here, :])
            low = (grad_act * slope[rel, :, here]).astype(BF)
            gup_out[rel, :, here] = low
            ups_out[rel : rel + 1, here] = col_sum(low.astype(F32))

        total[...] += nt(gup_out[rel], u[...])
    grad = total[...]
    res1 = norm_pull(grad, normed1[...], inv1[...], rows_in[GAIN1 : GAIN1 + 1, :])
    res1_out[...] = res1
    low = res1.astype(BF)
    low_out[...] = low
    sums_out[0:1, :] = col_sum(grad * normed1[...])
    sums_out[1:2, :] = col_sum(grad)
    sums_out[2:3, :] = col_sum(low.astype(F32))
    for rel, o in enumerate((o0, o1, o2, o3)):
        gm_out[rel] = nt(low, o[...]).astype(BF)


def backward(low2, res2, normed1, inv1, slope, downs, ups, outs, rows_in, after=()):
    rows, width = low2.shape
    hidden = slope.shape[2]
    cols = outs[0].shape[0]
    return call(
        backward_body,
        [
            ((4, rows, hidden), BF),
            ((rows, width), F32),
            ((rows, width), BF),
            ((4, rows, cols), BF),
            ((3, width), F32),
            ((4, hidden), F32),
        ],
        [VMEM] * 18,
        "backward",
        (low2, res2, normed1, inv1, slope, *downs, *ups, *outs, rows_in),
        after,
        scratch=[pltpu.VMEM((rows, width), F32)],
    )


def weight_grads_body(low1, gup, grad_low, m0, m1, m2, m3, keep_out, send_out):
    cols = m0.shape[1]
    for rel, m in enumerate((m0, m1, m2, m3)):
        out = send_out if rel % 2 else keep_out
        out[rel // 2, 0:cols, :] = tn(m[...], grad_low[...]).astype(BF)
        out[rel // 2, cols:, :] = tn(low1[...], gup[rel]).astype(BF)


def weight_grads(low1, gup, grad_low, mixed, after=()):
    width, hidden = low1.shape[1], gup.shape[2]
    cols = mixed[0].shape[1]
    return call(
        weight_grads_body,
        [((2, cols + width, hidden), BF), ((2, cols + width, hidden), BF)],
        [VMEM] * 7,
        "weight_grads",
        (low1, gup, grad_low, *mixed),
        after,
    )


def place_rows_body(place, p0, p1, p2, p3, out):
    quarter = p0.shape[0]
    for rel, p in enumerate((p0, p1, p2, p3)):
        here = pl.ds(pl.multiple_of((place[0] ^ rel) * quarter, quarter), quarter)
        out[here, :] = p[...].astype(out.dtype)


def place_rows(place, parts, dtype):
    quarter, width = parts[0].shape
    return call(
        place_rows_body,
        [((4 * quarter, width), dtype)],
        [SMEM] + [VMEM] * 4,
        "place_rows",
        (place, *parts),
    )[0]


def swap(value, axis, bits):
    count = lax.axis_size(axis)
    return lax.ppermute(value, axis, [(i, i ^ bits) for i in range(count)])


def gather_rel(own):
    far = swap(own, "tp", 2)
    return (own, swap(own, "tp", 1), far, swap(far, "tp", 1))


def core_sum(keep, send):
    two = keep.astype(F32) + swap(send, "tp", 1).astype(F32)
    return two[0], two[1].astype(BF)


def chip_sum(pair):
    return pair[0] + swap(pair[1], "tp", 2).astype(F32)


def sum_over_seq(part):
    count = lax.axis_size("seq")
    place = lax.axis_index("seq")
    bits = [1 << k for k in range(count.bit_length() - 1)]
    halved = bits[:3]
    for bit in halved:
        half = part.shape[0] // 2
        upper = (place & bit) != 0
        low, high = part[:half], part[half:]
        send = jnp.where(upper, low, high).astype(BF)
        keep = jnp.where(upper, high, low)
        part = keep + swap(send, "seq", bit).astype(F32)
    for bit in bits[3:]:
        mine = part.astype(BF)
        part = mine.astype(F32) + swap(mine, "seq", bit).astype(F32)
    part = part.astype(BF)
    for bit in halved[::-1]:
        other = swap(part, "seq", bit)
        upper = (place & bit) != 0
        part = jnp.concatenate(
            [jnp.where(upper, other, part), jnp.where(upper, part, other)], 0
        )
    return part.astype(F32)


def on_device(
    tokens, cotangent, lengths, w_qkv, qv_bias, w_out, out_bias, gain_first, shift_first,
    w_up, up_bias, w_down, down_bias, gain_second, shift_second,
):
    rows, width = tokens.shape
    quarter = rows // 4
    cols = w_qkv.shape[2]
    hidden = w_up.shape[1]
    seq_count = lax.axis_size("seq")
    tp_place = lax.axis_index("tp")
    seq_place = lax.axis_index("seq")
    place = tp_place.astype(jnp.int32).reshape(1)
    forwards = [(i, i + 1) for i in range(seq_count - 1)]
    backwards = [(b, a) for a, b in forwards]

    low = lax.ppermute(tokens[rows - MOST :], "seq", forwards)
    high = lax.ppermute(tokens[:MOST], "seq", backwards)
    outs = gather_rel(w_out)
    ups = gather_rel(w_up)
    downs = gather_rel(w_down)
    own_bias = up_bias.reshape(1, -1)
    chip_bias = jnp.concatenate([own_bias, swap(own_bias, "tp", 1)], 0)
    up_rows = jnp.concatenate([chip_bias, swap(chip_bias, "tp", 2)], 0)
    zero = jnp.zeros_like(out_bias)
    rows_in = jnp.stack(
        [out_bias, gain_first, shift_first, down_bias, gain_second, shift_second, zero, zero]
    )

    places = seq_place * rows + jnp.arange(rows + 2 * MOST, dtype=jnp.int32) - MOST
    ends = jnp.cumsum(lengths)
    passed = jnp.sum((ends[None, :] <= places[:, None]).astype(jnp.int32), 1)
    ids = jnp.where((places < 0) | (places >= rows * seq_count), -1, passed)

    wt = jnp.transpose(w_qkv, (0, 2, 1))
    q, k, v, probs, mixed = attend(
        place, tokens, low, high, wt, qv_bias, ids[:, None], ids[None, :]
    )
    mixed = [mixed[0]] + [swap(mixed[r], "tp", r) for r in (1, 2, 3)]

    here = tp_place * quarter
    tokens_here = lax.dynamic_slice_in_dim(tokens, here, quarter, 0)
    cot_here = lax.dynamic_slice_in_dim(cotangent, here, quarter, 0)
    normed1, inv1, low1, act, slope = forward(tokens_here, mixed, outs, ups, up_rows, rows_in)
    result, res2, low2, keep_d, send_d, sums2 = middle(normed1, act, downs, cot_here, rows_in)
    result = gather_rel(result)
    pair_d = core_sum(keep_d, send_d)
    gup, res1, grad_low, gm, sums1, up_sums = backward(
        low2, res2, normed1, inv1, slope, downs, ups, outs, rows_in
    )
    gm = [gm[0]] + [swap(gm[r], "tp", r) for r in (1, 2, 3)]
    keep_u, send_u = weight_grads(low1, gup, grad_low, mixed, pair_d)
    pair_u = core_sum(keep_u, send_u)
    dq, dk, dv = attend_back(place, q, k, v, probs, gm, pair_u)
    part_d = chip_sum(pair_d)

    pair = jnp.stack([dk, dv])
    to_low = lax.ppermute(pair[:, :MOST].astype(BF), "seq", backwards).astype(F32)
    to_high = lax.ppermute(pair[:, rows + MOST :].astype(BF), "seq", forwards).astype(F32)
    own = pair[:, MOST : rows + MOST]
    own = jnp.concatenate(
        [own[:, :MOST] + to_high, own[:, MOST : rows - MOST], own[:, rows - MOST :] + to_low], 1
    ).astype(BF)
    dk, dv = own[0], own[1]
    dwt, keep_i, send_i = project_back(place, tokens, dq, dk, dv, wt, (part_d,))
    grad_qkv = sum_over_seq(dwt.reshape(3 * cols, width)).reshape(3, cols, width)
    grad_qkv = jnp.transpose(grad_qkv, (0, 2, 1))
    grad_down = sum_over_seq(part_d)
    grad_bundle = sum_over_seq(chip_sum(pair_u))
    input_part = lax.optimization_barrier((chip_sum(core_sum(keep_i, send_i)) + res1).astype(BF))
    input_grad = place_rows(place, gather_rel(input_part), F32)
    result = place_rows(place, result, BF)

    sums = jnp.concatenate([sums2, sums1], 0)
    other = swap(jnp.concatenate([sums, up_sums[1::2]], 0), "tp", 1)
    sums, up_sums = sums + other[:6], up_sums[0::2] + other[6:]
    other = swap(jnp.concatenate([sums, up_sums[1:]], 0), "tp", 2)
    sums, up_sums = sums + other[:6], up_sums[:1] + other[6:]
    qv_sums = jnp.stack([jnp.sum(dq.astype(F32), 0), jnp.sum(dv.astype(F32), 0)])
    qv_row = jnp.pad(qv_sums.reshape(1, -1), ((0, 0), (0, width - 2 * cols)))
    sums = jnp.concatenate([sums, up_sums, qv_row], 0)
    for k in range(seq_count.bit_length() - 1):
        sums = sums + swap(sums, "seq", 1 << k)
    qv_sums = sums[7, : 2 * cols].reshape(2, cols)
    return (
        result, input_grad, grad_qkv, qv_sums, grad_bundle[:cols], sums[5], sums[3], sums[4],
        grad_bundle[cols:], sums[6], grad_down, sums[2], sums[0], sums[1],
    )


def solution(mesh):
    rep, rows = P(), P("seq", None)
    return jax.shard_map(
        on_device,
        mesh=mesh,
        in_specs=(
            rows, rows, rep, P(None, None, "tp"), P(None, "tp"), P("tp", None), rep, rep, rep,
            P(None, "tp"), P("tp"), P("tp", None), rep, rep, rep,
        ),
        out_specs=(
            rows, rows, P(None, None, "tp"), P(None, "tp"), P("tp", None), rep, rep, rep,
            P(None, "tp"), P("tp"), P("tp", None), rep, rep, rep,
        ),
        check_vma=False,
    )
```

time: 1000 us -> 381 us (0.38)
  waiting for transfers between devices: 657 us -> 134 us
  matrix products: 153 us -> 0 us
  Pallas kernels: 0 us -> 116 us
  starting transfers between devices: 12.2 us -> 60.4 us
  blocking collectives: 36.7 us -> 0 us
  local copies, waits for them, and re-layouts: 59 us -> 26.4 us
  other arithmetic: 59.1 us -> 35.6 us
  between operations: 14.5 us -> 1.94 us
    psum x5 -> x0, waiting for transfers between devices: 654 us -> none  [the longest x1 233 us: on_device(): lax.psum((grad_qkv, grad_qv_bias, grad_out, grad_out_bias, grad_gain1, gr...]
    ppermute x4 -> x56, waiting for transfers between devices: 2.88 us -> 134 us  [the longest x52 129 us: swap(): return lax.ppermute(value, axis, [(i, i ^ bits) for i in range(count)])]
    pallas_call x0 -> x9, Pallas kernels: none -> 116 us  [call(): pl.pallas_call(whole, out_shape=[jax.ShapeDtypeStruct(shape, dtype) for s...]
    dot_general x34 -> x0, matrix products: 115 us -> none  [the longest x6 36.1 us: product(): return jnp.dot(left, right, preferred_element_type=jnp.float32)]
    ppermute x4 -> x56, starting transfers between devices: 10.8 us -> 60.4 us  [the longest x52 48.4 us: swap(): return lax.ppermute(value, axis, [(i, i ^ bits) for i in range(count)])]
    sub x8 -> x0, matrix products: 38.1 us -> none  [attention_weights(): raised = jnp.exp(scores - row_max)]
    psum x1 -> x0, blocking collectives: 36.7 us -> none  [on_device(): lax.psum((grad_qkv, grad_qv_bias, grad_out, grad_out_bias, grad_gain1, gr...]
    reduce_sum x11 -> x3, other arithmetic: 37 us -> 2.01 us  [the longest x1 1.43 us: on_device(): passed = jnp.sum((ends[None, :] <= places[:, None]).astype(jnp.int32), 1)]
  transfers between devices with their start and end apart: 9 -> 56, of which waited for: 6 -> 24; matrix products, arithmetic and copies ran while one was open for 4% -> 13% of each run, Pallas kernels for 0% -> 27%
where the time goes in v1:
time: 381 us; the launch traced here: 374 us
  waiting for transfers between devices  134 us (35%)
  Pallas kernels  116 us (30%)
  starting transfers between devices  60.4 us (16%)
  other arithmetic  35.6 us (9%)
  local copies, waits for them, and re-layouts  26.4 us (7%)
    ppermute x52, waiting for transfers between devices, swap(): return lax.ppermute(value, axis, [(i, i ^ bits) for i in range(count)])  129 us
    pallas_call x9, Pallas kernels, call(): pl.pallas_call(whole, out_shape=[jax.ShapeDtypeStruct(shape, dtype) for s...  116 us
    ppermute x52, starting transfers between devices, swap(): return lax.ppermute(value, axis, [(i, i ^ bits) for i in range(count)])  48.4 us
  transfers between devices with their start and end apart: 56, of which 24 were waited for; matrix products, arithmetic and copies ran while one was open for 13% of the time, Pallas kernels for 27%

profile of v1, /device:TPU:0, one launch (start us, length us, event | category | flops | bytes accessed | tf_op | source)
XLA Modules:
  0.0 374.1 jit_solution(17581861894980048256)
XLA Ops:
  5.0 5.8 %collective-permute-start = (bf16[128,768]{1,0:T(8,128)(2,1)}, bf16[128,768]{1,0:T(8,128)(2,1)}, u32[]{:S(2)}, u32[]{:S(2)}) collective-permute-start(bf16[128,768]{1,0:T(8,128)(2,1)} %get-tuple-element.84), channel_id=1, source_target_pairs={{0,4},{4,8},{8,12},{12,16},{16,20},{20,24},{24,28},{1,5},{5,9},{9,... | collective-permute-start | bytes 589832 | tf_op jit(solution)/shard_map/ppermute | solution.py:474
  20.5 21.9 %attend.1 = (bf16[2048,192]{1,0:T(8,128)(2,1)}, bf16[2304,192]{1,0:T(8,128)(2,1)}, bf16[2304,192]{1,0:T(8,128)(2,1)}, bf16[16,384,384]{2,1,0:T(8,128)(2,1)}, bf16[4,512,192]{2,1,0:T(8,128)(2,1)}) custom-call(s32[1]{0:T(128)} %bitcast.refs_0_, bf16[2048,768]{1,0:T(8,128)(2,1)} %refs_1_.3, bf16[128,768]{1,0:T(8,128)(2,1)} %collective-permute-done.refs_2_, ...), custom_call_target="tpu_custom_call" | custom-call | tf_op jit(solution)/shard_map/attend/pallas_call | solution.py:41
  42.5 28.4 %collective-permute-done.12 = f32[2,768]{1,0:T(2,128)S(1)} collective-permute-done((f32[2,768]{1,0:T(2,128)S(1)}, f32[2,768]{1,0:T(2,128)S(1)}, u32[]{:S(2)}, u32[]{:S(2)}) %collective-permute-start.12) | collective-permute-done | bytes 6176 | tf_op jit(solution)/shard_map/ppermute | solution.py:417
  75.3 7.0 %collective-permute-done.4.refs_4_.refs_6_ = bf16[512,192]{1,0:T(8,128)(2,1)} collective-permute-done((bf16[512,192]{1,0:T(8,128)(2,1)S(1)}, bf16[512,192]{1,0:T(8,128)(2,1)}, u32[]{:S(2)}, u32[]{:S(2)}) %collective-permute-start.4) | collective-permute-done | bytes 196640 | tf_op jit(solution)/shard_map/ppermute | solution.py:417
  84.1 6.7 %collective-permute-done.3.refs_3_.refs_5_ = bf16[512,192]{1,0:T(8,128)(2,1)} collective-permute-done((bf16[512,192]{1,0:T(8,128)(2,1)S(1)}, bf16[512,192]{1,0:T(8,128)(2,1)}, u32[]{:S(2)}, u32[]{:S(2)}) %collective-permute-start.3) | collective-permute-done | bytes 196640 | tf_op jit(solution)/shard_map/ppermute | solution.py:417
  97.2 17.8 %forward.1 = (f32[512,768]{1,0:T(8,128)}, f32[512,1]{1,0:T(8,128)}, bf16[512,768]{1,0:T(8,128)(2,1)}, bf16[4,512,768]{2,1,0:T(8,128)(2,1)}, f32[4,512,768]{2,1,0:T(8,128)}) custom-call(bf16[512,768]{1,0:T(8,128)(2,1)} %constant_dynamic-slice_fusion.1.refs_0_, bf16[512,192]{1,0:T(8,128)(2,1)} %get-tuple-element.100.refs_1_.refs_3_, ...), custom_call_target="tpu_custom_call" | custom-call | tf_op jit(solution)/shard_map/forward/pallas_call | solution.py:41
  115.0 13.1 %middle.1 = (bf16[512,768]{1,0:T(8,128)(2,1)}, f32[512,768]{1,0:T(8,128)}, bf16[512,768]{1,0:T(8,128)(2,1)}, bf16[2,768,768]{2,1,0:T(8,128)(2,1)}, bf16[2,768,768]{2,1,0:T(8,128)(2,1)}, /*index=5*/f32[3,768]{1,0:T(4,128)}) custom-call(f32[512,768]{1,0:T(8,128)} %get-tuple-element.45.refs_0_.refs_2_, bf16[4,512,768]{2,1,0:T(8,128)(2,1)} %get-tuple-element.46.refs_1_, ...), custom_call_target="tpu_custom_call" | custom-call | tf_op jit(solution)/shard_map/middle/pallas_call | solution.py:41
  128.5 4.4 %collective-permute-done.22 = bf16[2,768,768]{2,1,0:T(8,128)(2,1)S(1)} collective-permute-done((bf16[2,768,768]{2,1,0:T(8,128)(2,1)}, bf16[2,768,768]{2,1,0:T(8,128)(2,1)S(1)}, u32[]{:S(2)}, u32[]{:S(2)}) %collective-permute-start.22) | collective-permute-done | bytes 2359328 | tf_op jit(solution)/shard_map/ppermute | solution.py:417
  140.4 18.0 %backward.1 = (bf16[4,512,768]{2,1,0:T(8,128)(2,1)}, f32[512,768]{1,0:T(8,128)}, bf16[512,768]{1,0:T(8,128)(2,1)}, bf16[4,512,192]{2,1,0:T(8,128)(2,1)}, f32[3,768]{1,0:T(4,128)}, /*index=5*/f32[4,768]{1,0:T(4,128)}) custom-call(bf16[512,768]{1,0:T(8,128)(2,1)} %get-tuple-element.52.refs_0_, f32[512,768]{1,0:T(8,128)} %get-tuple-element.53.refs_1_, ...), custom_call_target="tpu_custom_call" | custom-call | tf_op jit(solution)/shard_map/backward/pallas_call | solution.py:41
  159.2 3.4 slice_bitcast_fusion.1.refs_7_
  162.5 8.2 %weight_grads.1 = (bf16[2,960,768]{2,1,0:T(8,128)(2,1)}, bf16[2,960,768]{2,1,0:T(8,128)(2,1)}) custom-call(bf16[512,768]{1,0:T(8,128)(2,1)} %get-tuple-element.57.refs_0_, bf16[4,512,768]{2,1,0:T(8,128)(2,1)} %get-tuple-element.58.refs_1_, bf16[512,768]{1,0:T(8,128)(2,1)} %get-tuple-element.59.refs_2_, bf16[512,192]{1,0:T(8,128)(2,1)} %get-tuple-element.100.refs_1_.refs_3_, ...), custom_call_target="tpu_custom_call" | custom-call | tf_op jit(solution)/shard_map/weight_grads/pallas_call | solution.py:41
  177.5 11.8 %collective-permute-done.50 = bf16[384,768]{1,0:T(8,128)(2,1)} collective-permute-done((bf16[384,768]{1,0:T(8,128)(2,1)}, bf16[384,768]{1,0:T(8,128)(2,1)}, u32[]{:S(2)}, u32[]{:S(2)}) %collective-permute-start.50) | collective-permute-done | bytes 589856 | tf_op jit(solution)/shard_map/ppermute | solution.py:417
  193.2 5.8 %collective-permute-done.51 = bf16[192,768]{1,0:T(8,128)(2,1)S(1)} collective-permute-done((bf16[192,768]{1,0:T(8,128)(2,1)S(1)}, bf16[192,768]{1,0:T(8,128)(2,1)S(1)}, u32[]{:S(2)}, u32[]{:S(2)}) %collective-permute-start.51) | collective-permute-done | bytes 294944 | tf_op jit(solution)/shard_map/ppermute | solution.py:417
  199.1 2.8 collective-permute-start.52
  201.9 7.7 %collective-permute-done.52 = bf16[96,768]{1,0:T(8,128)(2,1)S(1)} collective-permute-done((bf16[96,768]{1,0:T(8,128)(2,1)S(1)}, bf16[96,768]{1,0:T(8,128)(2,1)S(1)}, u32[]{:S(2)}, u32[]{:S(2)}) %collective-permute-start.52) | collective-permute-done | bytes 147488 | tf_op jit(solution)/shard_map/ppermute | solution.py:417
  211.5 4.0 %place_rows.2 = bf16[2048,768]{1,0:T(8,128)(2,1)} custom-call(s32[1]{0:T(128)} %bitcast.refs_0_, bf16[512,768]{1,0:T(8,128)(2,1)} %get-tuple-element.47.refs_1_, bf16[512,768]{1,0:T(8,128)(2,1)} %collective-permute-done.16.refs_2_, bf16[512,768]{1,0:T(8,128)(2,1)} %collective-permute-done.17.refs_3_, bf16[512,768]{1,0:T(8,128)(2,1)} %copy-done.25), custom_call_target="tpu_custom_call" | custom-call | tf_op jit(solution)/shard_map/place_rows/pallas_call | solution.py:41
  215.5 3.9 %collective-permute-done.53 = bf16[96,768]{1,0:T(8,128)(2,1)S(1)} collective-permute-done((bf16[96,768]{1,0:T(8,128)(2,1)S(1)}, bf16[96,768]{1,0:T(8,128)(2,1)S(1)}, u32[]{:S(2)}, u32[]{:S(2)}) %collective-permute-start.53) | collective-permute-done | bytes 147488 | tf_op jit(solution)/shard_map/ppermute | solution.py:417
  227.5 18.4 %attend_back.1 = (bf16[2048,192]{1,0:T(8,128)(2,1)}, f32[2304,192]{1,0:T(8,128)}, f32[2304,192]{1,0:T(8,128)}) custom-call(s32[1]{0:T(128)} %bitcast.refs_0_, bf16[2048,192]{1,0:T(8,128)(2,1)} %get-tuple-element.48.refs_1_, bf16[2304,192]{1,0:T(8,128)(2,1)} %get-tuple-element.49.refs_2_, bf16[2304,192]{1,0:T(8,128)(2,1)} %get-tuple-element.50.refs_3_, ...), custom_call_target="tpu_custom_call" | custom-call | tf_op jit(solution)/shard_map/attend_back/pallas_call | solution.py:41
  245.8 2.8 fusion
  248.7 3.4 collective-permute-start.24
  255.0 4.1 %collective-permute-done.25 = bf16[2,128,192]{2,1,0:T(8,128)(2,1)S(1)} collective-permute-done((bf16[2,128,192]{2,1,0:T(8,128)(2,1)S(1)}, bf16[2,128,192]{2,1,0:T(8,128)(2,1)S(1)}, u32[]{:S(2)}, u32[]{:S(2)}) %collective-permute-start.25) | collective-permute-done | bytes 98336 | tf_op jit(solution)/shard_map/ppermute | solution.py:515
  263.9 9.7 %project_back.1 = (f32[3,192,768]{2,1,0:T(8,128)}, f32[2,512,768]{2,1,0:T(8,128)}, bf16[2,512,768]{2,1,0:T(8,128)(2,1)}) custom-call(s32[1]{0:T(128)} %bitcast.refs_0_, bf16[2048,768]{1,0:T(8,128)(2,1)} %refs_1_.3, bf16[2048,192]{1,0:T(8,128)(2,1)} %get-tuple-element.64.refs_2_, bf16[2048,192]{1,0:T(8,128)(2,1)} %get-tuple-element.88.refs_3_, ...), custom_call_target="tpu_custom_call" | custom-call | tf_op jit(solution)/shard_map/project_back/pallas_call | solution.py:41
  285.4 3.6 collective-permute-done.32
  290.1 2.6 convert_add_fusion.3
  298.1 5.9 %collective-permute-done.34 = bf16[72,768]{1,0:T(8,128)(2,1)S(1)} collective-permute-done((bf16[72,768]{1,0:T(8,128)(2,1)S(1)}, bf16[72,768]{1,0:T(8,128)(2,1)S(1)}, u32[]{:S(2)}, u32[]{:S(2)}) %collective-permute-start.34) | collective-permute-done | bytes 110624 | tf_op jit(solution)/shard_map/ppermute | solution.py:417
  304.1 10.0 %collective-permute-done.44 = bf16[480,768]{1,0:T(8,128)(2,1)S(1)} collective-permute-done((bf16[480,768]{1,0:T(8,128)(2,1)S(1)}, bf16[480,768]{1,0:T(8,128)(2,1)S(1)}, u32[]{:S(2)}, u32[]{:S(2)}) %collective-permute-start.44) | collective-permute-done | bytes 737312 | tf_op jit(solution)/shard_map/ppermute | solution.py:417
  319.1 3.0 collective-permute-done.45
  326.5 5.9 %collective-permute-done.46 = bf16[120,768]{1,0:T(8,128)(2,1)S(1)} collective-permute-done((bf16[120,768]{1,0:T(8,128)(2,1)S(1)}, bf16[120,768]{1,0:T(8,128)(2,1)S(1)}, u32[]{:S(2)}, u32[]{:S(2)}) %collective-permute-start.46) | collective-permute-done | bytes 184352 | tf_op jit(solution)/shard_map/ppermute | solution.py:417
  339.1 4.6 %collective-permute-start.48 = (bf16[240,768]{1,0:T(8,128)(2,1)S(1)}, bf16[240,768]{1,0:T(8,128)(2,1)S(1)}, u32[]{:S(2)}, u32[]{:S(2)}) collective-permute-start(bf16[240,768]{1,0:T(8,128)(2,1)S(1)} %pad_maximum_fusion.7), channel_id=1, source_target_pairs={{0,8},{4,12},{8,0},{12,4},{16,24},{20,28},{24,16},{28,20},{1,9},{5... | collective-permute-start | bytes 1105928 | tf_op jit(solution)/shard_map/ppermute | solution.py:417
  345.3 5.9 %collective-permute-done.30.refs_3_ = bf16[512,768]{1,0:T(8,128)(2,1)S(1)} collective-permute-done((bf16[512,768]{1,0:T(8,128)(2,1)S(1)}, bf16[512,768]{1,0:T(8,128)(2,1)S(1)}, u32[]{:S(2)}, u32[]{:S(2)}) %collective-permute-start.30) | collective-permute-done | bytes 786464 | tf_op jit(solution)/shard_map/ppermute | solution.py:417
  358.8 5.0 %place_rows.3 = f32[2048,768]{1,0:T(8,128)} custom-call(s32[1]{0:T(128)} %bitcast.refs_0_, bf16[512,768]{1,0:T(8,128)(2,1)} %copy-done.11, bf16[512,768]{1,0:T(8,128)(2,1)} %copy-done.23, bf16[512,768]{1,0:T(8,128)(2,1)} %copy-done.22, bf16[512,768]{1,0:T(8,128)(2,1)} %copy-done.24), custom_call_target="tpu_custom_call" | custom-call | tf_op jit(solution)/shard_map/place_rows/pallas_call | solution.py:41
  363.7 7.2 %collective-permute-done.49 = bf16[480,768]{1,0:T(8,128)(2,1)S(1)} collective-permute-done((bf16[480,768]{1,0:T(8,128)(2,1)S(1)}, bf16[480,768]{1,0:T(8,128)(2,1)S(1)}, u32[]{:S(2)}, u32[]{:S(2)}) %collective-permute-start.49) | collective-permute-done | bytes 737312 | tf_op jit(solution)/shard_map/ppermute | solution.py:417
  (271 shorter events, 109.8 us)
Async XLA Ops:
  1.5 16.0 %collective-permute-start.11 = (f32[1,768]{1,0:T(1,128)S(1)}, f32[1,768]{1,0:T(1,128)S(1)}, u32[]{:S(2)}, u32[]{:S(2)}) collective-permute-start(f32[1,768]{1,0:T(1,128)S(1)} %reshape.128), channel_id=1, source_target_pairs={{0,1},{1,0},{2,3},{3,2},{4,5},{5,4},{6,7},{7,6},{8,9},{9,8},{10,11... | collective-permute-start | bytes 9224 | tf_op jit(solution)/shard_map/ppermute | solution.py:417
  3.7 15.8 %collective-permute-start.1 = (bf16[128,768]{1,0:T(8,128)(2,1)}, bf16[128,768]{1,0:T(8,128)(2,1)}, u32[]{:S(2)}, u32[]{:S(2)}) collective-permute-start(bf16[128,768]{1,0:T(8,128)(2,1)} %get-tuple-element.83), channel_id=1, source_target_pairs={{4,0},{8,4},{12,8},{16,12},{20,16},{24,20},{28,24},{5,1},{9,5},{13... | collective-permute-start | bytes 589832 | tf_op jit(solution)/shard_map/ppermute | solution.py:475
  5.0 14.6 %collective-permute-start = (bf16[128,768]{1,0:T(8,128)(2,1)}, bf16[128,768]{1,0:T(8,128)(2,1)}, u32[]{:S(2)}, u32[]{:S(2)}) collective-permute-start(bf16[128,768]{1,0:T(8,128)(2,1)} %get-tuple-element.84), channel_id=1, source_target_pairs={{0,4},{4,8},{8,12},{12,16},{16,20},{20,24},{24,28},{1,5},{5,9},{9,... | collective-permute-start | bytes 589832 | tf_op jit(solution)/shard_map/ppermute | solution.py:474
  10.8 60.5 %collective-permute-start.9 = (bf16[768,768]{1,0:T(8,128)(2,1)}, bf16[768,768]{1,0:T(8,128)(2,1)}, u32[]{:S(2)}, u32[]{:S(2)}) collective-permute-start(bf16[768,768]{1,0:T(8,128)(2,1)} %refs_9_.3), channel_id=1, source_target_pairs={{0,2},{1,3},{2,0},{3,1},{4,6},{5,7},{6,4},{7,5},{8,10},{9,11},{10,... | collective-permute-start | bytes 3538952 | tf_op jit(solution)/shard_map/ppermute | solution.py:417
  12.9 58.5 %collective-permute-start.14 = (bf16[768,768]{1,0:T(8,128)(2,1)}, bf16[768,768]{1,0:T(8,128)(2,1)}, u32[]{:S(2)}, u32[]{:S(2)}) collective-permute-start(bf16[768,768]{1,0:T(8,128)(2,1)} %refs_5_.5), channel_id=1, source_target_pairs={{0,2},{1,3},{2,0},{3,1},{4,6},{5,7},{6,4},{7,5},{8,10},{9,11},{10,... | collective-permute-start | bytes 3538952 | tf_op jit(solution)/shard_map/ppermute | solution.py:417
  17.5 53.3 %collective-permute-start.6 = (bf16[192,768]{1,0:T(8,128)(2,1)}, bf16[192,768]{1,0:T(8,128)(2,1)S(1)}, u32[]{:S(2)}, u32[]{:S(2)}) collective-permute-start(bf16[192,768]{1,0:T(8,128)(2,1)} %refs_13_.1), channel_id=1, source_target_pairs={{0,2},{1,3},{2,0},{3,1},{4,6},{5,7},{6,4},{7,5},{8,10},{9,11},{10,... | collective-permute-start | bytes 884744 | tf_op jit(solution)/shard_map/ppermute | solution.py:417
  19.5 54.4 %collective-permute-start.5 = (bf16[192,768]{1,0:T(8,128)(2,1)}, bf16[192,768]{1,0:T(8,128)(2,1)}, u32[]{:S(2)}, u32[]{:S(2)}) collective-permute-start(bf16[192,768]{1,0:T(8,128)(2,1)} %refs_13_.1), channel_id=1, source_target_pairs={{0,1},{1,0},{2,3},{3,2},{4,5},{5,4},{6,7},{7,6},{8,9},{9,8},{10,11... | collective-permute-start | bytes 884744 | tf_op jit(solution)/shard_map/ppermute | solution.py:417
  19.6 51.2 %collective-permute-start.12 = (f32[2,768]{1,0:T(2,128)S(1)}, f32[2,768]{1,0:T(2,128)S(1)}, u32[]{:S(2)}, u32[]{:S(2)}) collective-permute-start(f32[2,768]{1,0:T(2,128)S(1)} %pad_maximum_fusion.13), channel_id=1, source_target_pairs={{0,2},{1,3},{2,0},{3,1},{4,6},{5,7},{6,4},{7,5},{8,10},{9,11},{10,... | collective-permute-start | bytes 18440 | tf_op jit(solution)/shard_map/ppermute | solution.py:417
  70.8 26.4 %collective-permute-start.8 = (bf16[768,768]{1,0:T(8,128)(2,1)}, bf16[768,768]{1,0:T(8,128)(2,1)}, u32[]{:S(2)}, u32[]{:S(2)}) collective-permute-start(bf16[768,768]{1,0:T(8,128)(2,1)} %refs_9_.3), channel_id=1, source_target_pairs={{0,1},{1,0},{2,3},{3,2},{4,5},{5,4},{6,7},{7,6},{8,9},{9,8},{10,11... | collective-permute-start | bytes 3538952 | tf_op jit(solution)/shard_map/ppermute | solution.py:417
  70.8 44.1 %collective-permute-start.13 = (bf16[768,768]{1,0:T(8,128)(2,1)}, bf16[768,768]{1,0:T(8,128)(2,1)}, u32[]{:S(2)}, u32[]{:S(2)}) collective-permute-start(bf16[768,768]{1,0:T(8,128)(2,1)} %refs_5_.5), channel_id=1, source_target_pairs={{0,1},{1,0},{2,3},{3,2},{4,5},{5,4},{6,7},{7,6},{8,9},{9,8},{10,11... | collective-permute-start | bytes 3538952 | tf_op jit(solution)/shard_map/ppermute | solution.py:417
  71.3 25.8 %collective-permute-start.10 = (bf16[768,768]{1,0:T(8,128)(2,1)}, bf16[768,768]{1,0:T(8,128)(2,1)}, u32[]{:S(2)}, u32[]{:S(2)}) collective-permute-start(bf16[768,768]{1,0:T(8,128)(2,1)} %collective-permute-done.9.refs_11_), channel_id=1, source_target_pairs={{0,1},{1,0},{2,3},{3,2},{4,5},{5,4},{6,7},{7,6},{8,9},{9,8},{10,11... | collective-permute-start | bytes 3538952 | tf_op jit(solution)/shard_map/ppermute | solution.py:417
  71.4 43.5 %collective-permute-start.15 = (bf16[768,768]{1,0:T(8,128)(2,1)}, bf16[768,768]{1,0:T(8,128)(2,1)}, u32[]{:S(2)}, u32[]{:S(2)}) collective-permute-start(bf16[768,768]{1,0:T(8,128)(2,1)} %collective-permute-done.14.refs_4_.refs_7_), channel_id=1, source_target_pairs={{0,1},{1,0},{2,3},{3,2},{4,5},{5,4},{6,7},{7,6},{8,9},{9,8},{10,11... | collective-permute-start | bytes 3538952 | tf_op jit(solution)/shard_map/ppermute | solution.py:417
  137.4 33.8 %collective-permute-start.26 = (bf16[768,768]{1,0:T(8,128)(2,1)S(1)}, bf16[768,768]{1,0:T(8,128)(2,1)}, u32[]{:S(2)}, u32[]{:S(2)}) collective-permute-start(bf16[768,768]{1,0:T(8,128)(2,1)S(1)} %fusion.5.refs_8_), channel_id=1, source_target_pairs={{0,2},{1,3},{2,0},{3,1},{4,6},{5,7},{6,4},{7,5},{8,10},{9,11},{10,... | collective-permute-start | bytes 3538952 | tf_op jit(solution)/shard_map/ppermute | solution.py:417
  139.2 53.1 %collective-permute-start.17 = (bf16[512,768]{1,0:T(8,128)(2,1)S(1)}, bf16[512,768]{1,0:T(8,128)(2,1)}, u32[]{:S(2)}, u32[]{:S(2)}) collective-permute-start(bf16[512,768]{1,0:T(8,128)(2,1)S(1)} %copy-done.21), channel_id=1, source_target_pairs={{0,2},{1,3},{2,0},{3,1},{4,6},{5,7},{6,4},{7,5},{8,10},{9,11},{10,... | collective-permute-start | bytes 2359304 | tf_op jit(solution)/shard_map/ppermute | solution.py:417
  140.4 69.4 %collective-permute-start.16 = (bf16[512,768]{1,0:T(8,128)(2,1)S(1)}, bf16[512,768]{1,0:T(8,128)(2,1)}, u32[]{:S(2)}, u32[]{:S(2)}) collective-permute-start(bf16[512,768]{1,0:T(8,128)(2,1)S(1)} %copy-done.21), channel_id=1, source_target_pairs={{0,1},{1,0},{2,3},{3,2},{4,5},{5,4},{6,7},{7,6},{8,9},{9,8},{10,11... | collective-permute-start | bytes 2359304 | tf_op jit(solution)/shard_map/ppermute | solution.py:417
  170.7 48.8 %collective-permute-start.23 = (bf16[2,960,768]{2,1,0:T(8,128)(2,1)}, bf16[2,960,768]{2,1,0:T(8,128)(2,1)}, u32[]{:S(2)}, u32[]{:S(2)}) collective-permute-start(bf16[2,960,768]{2,1,0:T(8,128)(2,1)} %get-tuple-element.63), channel_id=1, source_target_pairs={{0,1},{1,0},{2,3},{3,2},{4,5},{5,4},{6,7},{7,6},{8,9},{9,8},{10,11... | collective-permute-start | bytes 8847368 | tf_op jit(solution)/shard_map/ppermute | solution.py:417
  173.6 15.7 %collective-permute-start.50 = (bf16[384,768]{1,0:T(8,128)(2,1)}, bf16[384,768]{1,0:T(8,128)(2,1)}, u32[]{:S(2)}, u32[]{:S(2)}) collective-permute-start(bf16[384,768]{1,0:T(8,128)(2,1)} %select_convert_fusion.1), channel_id=1, source_target_pairs={{0,4},{4,0},{8,12},{12,8},{16,20},{20,16},{24,28},{28,24},{1,5},{5... | collective-permute-start | bytes 1769480 | tf_op jit(solution)/shard_map/ppermute | solution.py:417
  176.7 49.9 %collective-permute-start.21 = (bf16[512,192]{1,0:T(8,128)(2,1)}, bf16[512,192]{1,0:T(8,128)(2,1)S(1)}, u32[]{:S(2)}, u32[]{:S(2)}) collective-permute-start(bf16[512,192]{1,0:T(8,128)(2,1)} %get-tuple-element.93), channel_id=1, source_target_pairs={{0,3},{1,2},{2,1},{3,0},{4,7},{5,6},{6,5},{7,4},{8,11},{9,10},{10,... | collective-permute-start | bytes 589832 | tf_op jit(solution)/shard_map/ppermute | solution.py:417
  209.8 16.8 %collective-permute-start.20 = (bf16[512,192]{1,0:T(8,128)(2,1)}, bf16[512,192]{1,0:T(8,128)(2,1)S(1)}, u32[]{:S(2)}, u32[]{:S(2)}) collective-permute-start(bf16[512,192]{1,0:T(8,128)(2,1)} %get-tuple-element.94), channel_id=1, source_target_pairs={{0,2},{1,3},{2,0},{3,1},{4,6},{5,7},{6,4},{7,5},{8,10},{9,11},{10,... | collective-permute-start | bytes 589832 | tf_op jit(solution)/shard_map/ppermute | solution.py:417
  210.6 16.0 %collective-permute-start.19 = (bf16[512,192]{1,0:T(8,128)(2,1)}, bf16[512,192]{1,0:T(8,128)(2,1)S(1)}, u32[]{:S(2)}, u32[]{:S(2)}) collective-permute-start(bf16[512,192]{1,0:T(8,128)(2,1)} %get-tuple-element.95), channel_id=1, source_target_pairs={{0,1},{1,0},{2,3},{3,2},{4,5},{5,4},{6,7},{7,6},{8,9},{9,8},{10,11... | collective-permute-start | bytes 589832 | tf_op jit(solution)/shard_map/ppermute | solution.py:417
  219.4 58.2 %collective-permute-start.54 = (bf16[192,768]{1,0:T(8,128)(2,1)S(1)}, bf16[192,768]{1,0:T(8,128)(2,1)}, u32[]{:S(2)}, u32[]{:S(2)}) collective-permute-start(bf16[192,768]{1,0:T(8,128)(2,1)S(1)} %pad_maximum_fusion.8), channel_id=1, source_target_pairs={{0,8},{4,12},{8,0},{12,4},{16,24},{20,28},{24,16},{28,20},{1,9},{5... | collective-permute-start | bytes 884744 | tf_op jit(solution)/shard_map/ppermute | solution.py:417
  224.0 66.1 %collective-permute-start.43 = (bf16[960,768]{1,0:T(8,128)(2,1)}, bf16[960,768]{1,0:T(8,128)(2,1)}, u32[]{:S(2)}, u32[]{:S(2)}) collective-permute-start(bf16[960,768]{1,0:T(8,128)(2,1)} %fusion.4.refs_10_), channel_id=1, source_target_pairs={{0,2},{1,3},{2,0},{3,1},{4,6},{5,7},{6,4},{7,5},{8,10},{9,11},{10,... | collective-permute-start | bytes 4423688 | tf_op jit(solution)/shard_map/ppermute | solution.py:417
  261.4 14.7 %collective-permute-start.40 = (f32[8,768]{1,0:T(8,128)S(1)}, f32[8,768]{1,0:T(8,128)S(1)}, u32[]{:S(2)}, u32[]{:S(2)}) collective-permute-start(f32[8,768]{1,0:T(8,128)S(1)} %select_maximum_fusion), channel_id=1, source_target_pairs={{0,4},{4,0},{8,12},{12,8},{16,20},{20,16},{24,28},{28,24},{1,5},{5... | collective-permute-start | bytes 73736 | tf_op jit(solution)/shard_map/ppermute | solution.py:417
  276.1 13.0 %collective-permute-start.32 = (bf16[288,768]{1,0:T(8,128)(2,1)}, bf16[288,768]{1,0:T(8,128)(2,1)S(1)}, u32[]{:S(2)}, u32[]{:S(2)}) collective-permute-start(bf16[288,768]{1,0:T(8,128)(2,1)} %select_convert_fusion.2), channel_id=1, source_target_pairs={{0,4},{4,0},{8,12},{12,8},{16,20},{20,16},{24,28},{28,24},{1,5},{5... | collective-permute-start | bytes 1327112 | tf_op jit(solution)/shard_map/ppermute | solution.py:417
  282.2 61.4 %collective-permute-start.55 = (bf16[384,768]{1,0:T(8,128)(2,1)}, bf16[384,768]{1,0:T(8,128)(2,1)}, u32[]{:S(2)}, u32[]{:S(2)}) collective-permute-start(bf16[384,768]{1,0:T(8,128)(2,1)} %pad_maximum_fusion.5), channel_id=1, source_target_pairs={{0,4},{4,0},{8,12},{12,8},{16,20},{20,16},{24,28},{28,24},{1,5},{5... | collective-permute-start | bytes 1769480 | tf_op jit(solution)/shard_map/ppermute | solution.py:417
  283.4 32.5 %collective-permute-start.27 = (bf16[2,512,768]{2,1,0:T(8,128)(2,1)}, bf16[2,512,768]{2,1,0:T(8,128)(2,1)}, u32[]{:S(2)}, u32[]{:S(2)}) collective-permute-start(bf16[2,512,768]{2,1,0:T(8,128)(2,1)} %get-tuple-element.68), channel_id=1, source_target_pairs={{0,1},{1,0},{2,3},{3,2},{4,5},{5,4},{6,7},{7,6},{8,9},{9,8},{10,11... | collective-permute-start | bytes 4718600 | tf_op jit(solution)/shard_map/ppermute | solution.py:417
  292.8 21.4 %collective-permute-start.44 = (bf16[480,768]{1,0:T(8,128)(2,1)S(1)}, bf16[480,768]{1,0:T(8,128)(2,1)S(1)}, u32[]{:S(2)}, u32[]{:S(2)}) collective-permute-start(bf16[480,768]{1,0:T(8,128)(2,1)S(1)} %select_convert_fusion), channel_id=1, source_target_pairs={{0,4},{4,0},{8,12},{12,8},{16,20},{20,16},{24,28},{28,24},{1,5},{5... | collective-permute-start | bytes 2211848 | tf_op jit(solution)/shard_map/ppermute | solution.py:417
  304.0 20.6 %collective-permute-start.35 = (bf16[72,768]{1,0:T(8,128)(2,1)S(1)}, bf16[72,768]{1,0:T(8,128)(2,1)S(1)}, u32[]{:S(2)}, u32[]{:S(2)}) collective-permute-start(bf16[72,768]{1,0:T(8,128)(2,1)S(1)} %add_convert_fusion.2), channel_id=1, source_target_pairs={{0,16},{4,20},{8,24},{12,28},{16,0},{20,4},{24,8},{28,12},{1,17},{... | collective-permute-start | bytes 331784 | tf_op jit(solution)/shard_map/ppermute | solution.py:417
  317.8 17.4 %collective-permute-start.28 = (bf16[512,768]{1,0:T(8,128)(2,1)S(1)}, bf16[512,768]{1,0:T(8,128)(2,1)S(1)}, u32[]{:S(2)}, u32[]{:S(2)}) collective-permute-start(bf16[512,768]{1,0:T(8,128)(2,1)S(1)} %fusion.10), channel_id=1, source_target_pairs={{0,2},{1,3},{2,0},{3,1},{4,6},{5,7},{6,4},{7,5},{8,10},{9,11},{10,... | collective-permute-start | bytes 2359304 | tf_op jit(solution)/shard_map/ppermute | solution.py:417
  324.7 20.3 %collective-permute-start.36 = (bf16[144,768]{1,0:T(8,128)(2,1)S(1)}, bf16[144,768]{1,0:T(8,128)(2,1)S(1)}, u32[]{:S(2)}, u32[]{:S(2)}) collective-permute-start(bf16[144,768]{1,0:T(8,128)(2,1)S(1)} %pad_maximum_fusion.9), channel_id=1, source_target_pairs={{0,8},{4,12},{8,0},{12,4},{16,24},{20,28},{24,16},{28,20},{1,9},{5... | collective-permute-start | bytes 663560 | tf_op jit(solution)/shard_map/ppermute | solution.py:417
  335.5 15.7 %collective-permute-start.30 = (bf16[512,768]{1,0:T(8,128)(2,1)S(1)}, bf16[512,768]{1,0:T(8,128)(2,1)S(1)}, u32[]{:S(2)}, u32[]{:S(2)}) collective-permute-start(bf16[512,768]{1,0:T(8,128)(2,1)S(1)} %fusion.3.refs_1_), channel_id=1, source_target_pairs={{0,2},{1,3},{2,0},{3,1},{4,6},{5,7},{6,4},{7,5},{8,10},{9,11},{10,... | collective-permute-start | bytes 2359304 | tf_op jit(solution)/shard_map/ppermute | solution.py:417
  351.4 19.6 %collective-permute-start.49 = (bf16[480,768]{1,0:T(8,128)(2,1)S(1)}, bf16[480,768]{1,0:T(8,128)(2,1)S(1)}, u32[]{:S(2)}, u32[]{:S(2)}) collective-permute-start(bf16[480,768]{1,0:T(8,128)(2,1)S(1)} %pad_maximum_fusion.4), channel_id=1, source_target_pairs={{0,4},{4,0},{8,12},{12,8},{16,20},{20,16},{24,28},{28,24},{1,5},{5... | collective-permute-start | bytes 2211848 | tf_op jit(solution)/shard_map/ppermute | solution.py:417
  (65 other events, 843.7 us)
